TPU v7x, 256 devices: a whole 4x4x8 slice. The times are simulated.
256 devices in a mesh: inner: 16 (over z, y_hi), outer: 4 (over y_lo, core), heads: 4 (over x).
Axes of the slice: x: 4, y: 4 (y_hi: 2, y_lo: 2; y = y_hi * 2 + y_lo), z: 8, core: 2. Of those that a mesh axis runs over, the one named last changes fastest.
Arguments:
- query_states: bfloat16 [8192, 4096], P(('inner', 'outer'), 'heads'), parts along dimension 1, may hold values from -8 to 8
- key_states: bfloat16 [8192, 512], P(('inner', 'outer'), 'heads'), parts along dimension 1, may hold values from -4 to 4
- value_states: bfloat16 [8192, 512], P(('inner', 'outer'), 'heads'), parts along dimension 1, may hold values from -6 to 6
- output_grad: bfloat16 [8192, 4096], P(('inner', 'outer'), 'heads'), parts along dimension 1, may hold values from -2 to 2
- positions: int32 [8192], P(('inner', 'outer')), may hold values from 0 to 8191, as said below
Outputs:
- query_grad: bfloat16 [8192, 4096], P(('inner', 'outer'), 'heads'), parts along dimension 1
- key_grad: bfloat16 [8192, 512], P(('inner', 'outer'), 'heads'), parts along dimension 1
- value_grad: bfloat16 [8192, 512], P(('inner', 'outer'), 'heads'), parts along dimension 1
There are 4 independent parts, one for each index of `heads`. A program takes and returns all parts, laid end to end along the dimension named above; an argument that names none is the same for every part. Nothing has to cross between parts.
Inputs may be any that keep to these rules, and one draw needn't show every extreme that they name: Over all rows every position occurs once; each aligned block of 64 stored rows holds 64 consecutive positions in increasing order, the blocks in an order drawn from the seed.
All inputs are finite; a program needn't handle non-finite values.
Results may differ from a plain program's by a relative error of at most 0.017.
Values may be sent and summed in bfloat16 or wider, within the bound.
No kernel may reach another device: no remote copies, remote signals or barrier semaphores. Data moves between devices by JAX's collectives and lax.ppermute only.
A program may use at most 128 MiB of HBM per device.

v0:
```python
import jax
import jax.numpy as jnp
from jax import lax
from jax.sharding import PartitionSpec as P


def contract_last(left, right):
    return lax.dot_general(
        left, right, (((1,), (1,)), ((), ())), preferred_element_type=jnp.float32
    )


def contract_first(left, right):
    return lax.dot_general(
        left, right, (((0,), (0,)), ((), ())), preferred_element_type=jnp.float32
    )


def on_device(query_states, key_states, value_states, output_grad, positions):
    token_count = query_states.shape[0]
    head_size = key_states.shape[1]
    head_count = query_states.shape[1] // head_size
    row_count = token_count * head_count
    score_scale = head_size ** (-0.5)
    query_rows = query_states.reshape(row_count, head_size)
    grad_rows = output_grad.reshape(row_count, head_size)
    query_pos = jnp.repeat(positions, head_count)
    latest = jnp.max(positions)
    whole_rows = token_count * lax.axis_size("inner") * lax.axis_size("outer")
    start_fwd = (
        jnp.full((row_count,), -1e30, jnp.float32),
        jnp.zeros((row_count,), jnp.float32),
        jnp.zeros((row_count, head_size), jnp.float32),
    )
    key_part = lax.all_gather(key_states, ("inner", "outer"), axis=0, tiled=True)
    value_part = lax.all_gather(value_states, ("inner", "outer"), axis=0, tiled=True)
    key_pos = lax.all_gather(positions, ("inner", "outer"), axis=0, tiled=True)

    def forward_compute_tile(tile_state):
        run_max, run_total, run_acc = tile_state
        scores = contract_last(query_rows, key_part) * score_scale
        allowed = key_pos[None, :] <= query_pos[:, None]
        row_peak = jnp.max(jnp.where(allowed, scores, -jnp.inf), axis=1)
        new_max = jnp.maximum(run_max, row_peak)
        weights = jnp.where(allowed, jnp.exp(scores - new_max[:, None]), 0.0)
        run_total = jnp.sum(weights, axis=1)
        run_acc = jnp.dot(
            weights.astype(jnp.bfloat16), value_part, preferred_element_type=jnp.float32
        )
        return (new_max, run_total, run_acc)

    def forward_unchanged(tile_state):
        return tile_state

    run_max, run_total, run_acc = lax.cond(
        jnp.min(key_pos) <= latest, forward_compute_tile, forward_unchanged, start_fwd
    )
    attn_out = (run_acc / run_total[:, None]).astype(jnp.bfloat16)
    attn_out = lax.optimization_barrier(attn_out)
    log_rows = run_max + jnp.log(run_total)
    delta_rows = jnp.sum(grad_rows.astype(jnp.float32) * attn_out.astype(jnp.float32), axis=1)
    start_bwd = (
        jnp.zeros((row_count, head_size), jnp.float32),
        jnp.zeros((whole_rows, 2 * head_size), jnp.float32),
    )
    backward_key_part = lax.all_gather(key_states, ("inner", "outer"), axis=0, tiled=True)
    backward_value_part = lax.all_gather(value_states, ("inner", "outer"), axis=0, tiled=True)
    backward_key_pos = lax.all_gather(positions, ("inner", "outer"), axis=0, tiled=True)

    def backward_compute_tile(tile_state):
        scores = contract_last(query_rows, backward_key_part) * score_scale
        allowed = backward_key_pos[None, :] <= query_pos[:, None]
        attn_probs = jnp.where(allowed, jnp.exp(scores - log_rows[:, None]), 0.0)
        grad_probs = contract_last(grad_rows, backward_value_part)
        grad_scores = attn_probs * (grad_probs - delta_rows[:, None])
        probs_low = attn_probs.astype(jnp.bfloat16)
        scores_low = grad_scores.astype(jnp.bfloat16)
        key_term = contract_first(scores_low, query_rows) * score_scale
        value_term = contract_first(probs_low, grad_rows)
        query_acc = jnp.dot(scores_low, backward_key_part, preferred_element_type=jnp.float32)
        updated = jnp.concatenate([key_term, value_term], axis=1)
        return (query_acc, updated)

    def backward_unchanged(tile_state):
        return tile_state

    query_acc, pair_grads = lax.cond(
        jnp.min(backward_key_pos) <= latest, backward_compute_tile, backward_unchanged, start_bwd
    )
    own_sums = lax.psum_scatter(pair_grads, ("inner", "outer"), scatter_dimension=0, tiled=True)
    query_grad = (
        (query_acc * score_scale).astype(jnp.bfloat16).reshape(token_count, head_count * head_size)
    )
    key_grad = own_sums[:, :head_size].astype(jnp.bfloat16)
    value_grad = own_sums[:, head_size:].astype(jnp.bfloat16)
    return (query_grad, key_grad, value_grad)


def solution(mesh):
    in_specs = (
        P(("inner", "outer"), "heads"),
        P(("inner", "outer"), "heads"),
        P(("inner", "outer"), "heads"),
        P(("inner", "outer"), "heads"),
        P(("inner", "outer")),
    )
    out_specs = (
        P(("inner", "outer"), "heads"),
        P(("inner", "outer"), "heads"),
        P(("inner", "outer"), "heads"),
    )
    return jax.shard_map(
        on_device, mesh=mesh, in_specs=in_specs, out_specs=out_specs, check_vma=False
    )
```

profile of v0, /device:TPU:1, one launch (start us, length us, event | category | flops | bytes accessed | tf_op | source)
XLA Modules:
  0.0 452.3 jit_solution(2919252056574236587)
XLA Ops:
  7.2 0.0 all-gather.4.cloned.1.call-start
  7.2 0.7 all-gather.4.cloned.1.call-update
  7.9 0.0 all-gather.6.cloned.1.call-start
  7.9 0.7 all-gather.6.cloned.1.call-update
  8.6 0.0 reduce-scatter.2.cloned.1.call-start
  8.7 1.3 reduce_max.18
  10.0 44.2 %all-gather = s32[64,1,128]{2,1,0:T(1,128)S(1)} all-gather(s32[1,1,128]{2,1,0:T(1,128)} %bitcast.16), channel_id=1, replica_groups=mesh['inner'=16,'outer'=4,'heads'=4] {'inner','outer'}, dimensions={0}, use_global_device_ids=true | all-gather | bytes 33280 | tf_op jit(solution)/shard_map/all_gather | solution.py:68
  54.2 0.7 reduce_min.8
  56.2 1.1 reshape.27
  57.3 35.1 %all-gather.4.cloned.1.call-done = bf16[8192,128]{1,0:T(8,128)(2,1)} async-done(((bf16[128,128]{1,0:T(8,128)(2,1)}), bf16[8192,128]{1,0:T(8,128)(2,1)}) %all-gather.4.cloned.1.call-update) | async-done | bytes 2097168 | tf_op jit(solution)/shard_map/all_gather | solution.py:66
  92.3 77.8 %all-gather.6.cloned.1.call-done = bf16[8192,128]{1,0:T(8,128)(2,1)} async-done(((bf16[128,128]{1,0:T(8,128)(2,1)}), bf16[8192,128]{1,0:T(8,128)(2,1)}) %all-gather.6.cloned.1.call-update) | async-done | bytes 2097168 | tf_op jit(solution)/shard_map/all_gather | solution.py:36
  170.1 0.7 broadcast_in_dim.35
  170.8 0.0 copy-start.2
  170.8 46.2 %conditional.2 = (f32[1024]{0:T(1024)}, f32[1024]{0:T(1024)}, f32[1024,128]{1,0:T(8,128)S(1)}, f32[1024]{0:T(1024)S(1)}) conditional(s32[]{:T(128)} %convert_element_type.34, () %tuple.34, (s32[8192]{0:T(1024)S(1)}, s32[128,8]{1,0:T(8,128)S(1)}, bf16[1024,128]{1,0:T(8,128)(2,1)S(1)}, bf16[8192,128]{1,0:T(8,128)(2,1)}, ...), branch_computations={%region_2.0_spmd, %region_3.6_spmd} | conditional | flops 4412406784 | bytes 114184248 | solution.py:55
  170.8 0.0 copy-start.3
  170.9 0.1 le.34
  170.9 15.3 %fusion = (f32[1024]{0:T(1024)S(1)}, f32[1024,8192]{1,0:T(8,128)}) fusion(s32[8192]{0:T(1024)S(1)} %get-tuple-element.74, s32[1024]{0:T(1024)S(1)} %le.34, bf16[1024,128]{1,0:T(8,128)(2,1)S(1)} %get-tuple-element.76, bf16[8192,128]{1,0:T(8,128)(2,1)} %get-tuple-element.77), kind=kOutput, calls=%fused_computation.2 | convolution fusion | flops 2181037056 | bytes 35954688 | tf_op jit(solution)/shard_map/cond/branch_1_fun/dot_general | solution.py:8
  186.2 0.6 broadcast_maximum_fusion
  186.8 0.0 copy-done.3
  186.8 13.8 %fusion.3 = f32[1024,128]{1,0:T(8,128)S(1)} fusion(bf16[8192,128]{1,0:T(8,128)(2,1)S(1)} %copy-done.3, f32[1024,8192]{1,0:T(8,128)} %get-tuple-element.106, f32[1024]{0:T(1024)} %broadcast_maximum_fusion, s32[8192]{0:T(1024)S(1)} %get-tuple-element.74, s32[1024]{0:T(1024)S(1)} %le.34), kind=kOutput, calls=%fused_computation.5 | convolution fusion | flops 2189426688 | bytes 36216832 | tf_op jit(solution)/shard_map/cond/branch_1_fun/dot_general | solution.py:47
  200.7 15.7 %fusion.2 = f32[1024]{0:T(1024)} fusion(f32[1024,8192]{1,0:T(8,128)} %get-tuple-element.106, f32[1024]{0:T(1024)} %broadcast_maximum_fusion, s32[8192]{0:T(1024)S(1)} %get-tuple-element.74, s32[1024]{0:T(1024)S(1)} %le.34), kind=kLoop, calls=%fused_computation.4 | loop fusion | flops 41942016 | bytes 33599488 | tf_op jit(solution)/shard_map/cond/branch_1_fun/reduce_sum | solution.py:46
  216.4 0.7 log.5
  217.0 0.9 divide_convert_fusion
  218.0 0.0 copy-done.2
  218.0 73.1 %conditional.3 = (f32[1024,128]{1,0:T(8,128)S(1)}, f32[8192,256]{0,1:T(8,128)}) conditional(s32[]{:T(128)} %convert_element_type.34, () %tuple.33, (s32[8192]{0:T(1024)S(1)}, s32[128,8]{1,0:T(8,128)S(1)}, bf16[1024,128]{1,0:T(8,128)(2,1)S(1)}, bf16[8192,128]{1,0:T(8,128)(2,1)}, f32[1024]{0:T(1024)}, /*index=5*/f32[1024]{0:T(1024)S(1)}, ...), branch_computations={%region_6.7_spmd, %region_7.0_spmd} | conditional | flops 10841620480 | bytes 210612304 | solution.py:87
  218.0 0.1 le.38
  218.1 0.7 add.7
  218.8 0.1 reshape.24
  218.9 0.2 multiply_reduce_fusion
  219.1 14.9 %fusion.13 = f32[1024,8192]{1,0:T(8,128)} fusion(bf16[1024,128]{1,0:T(8,128)(2,1)S(1)} %get-tuple-element.81, bf16[8192,128]{1,0:T(8,128)(2,1)} %get-tuple-element.82), kind=kOutput, calls=%fused_computation.21 | convolution fusion | flops 2147483648 | bytes 35913728 | tf_op jit(solution)/shard_map/cond/branch_1_fun/dot_general | solution.py:8
  234.0 15.8 %fusion.8 = f32[8192,128]{0,1:T(8,128)} fusion(bf16[1024,128]{1,0:T(8,128)(2,1)S(1)} %reshape.24, f32[1024,8192]{1,0:T(8,128)} %fusion.13, f32[1024]{0:T(1024)S(1)} %add.7, s32[8192]{0:T(1024)S(1)} %get-tuple-element.79, s32[1024]{0:T(1024)S(1)} %le.38), kind=kOutput, calls=%fused_computation.12 | convolution fusion | flops 2189426688 | bytes 38051840 | tf_op jit(solution)/shard_map/cond/branch_1_fun/dot_general | solution.py:14
  249.8 0.0 copy-start.1
  249.8 20.8 %multiply_convert_fusion = bf16[1024,8192]{1,0:T(8,128)(2,1)} fusion(f32[1024,8192]{1,0:T(8,128)} %fusion.13, f32[1024]{0:T(1024)S(1)} %multiply_reduce_fusion, f32[1024]{0:T(1024)S(1)} %add.7, s32[8192]{0:T(1024)S(1)} %get-tuple-element.79, s32[1024]{0:T(1024)S(1)} %le.38, bf16[1024,128]{1,0:T(8,128)(2,1)S(1)} %reshape.24, ...), kind=kOutput, calls=%fused_computation.9 | convolution fusion | flops 2206203904 | bytes 52736000 | tf_op jit(solution)/shard_map/cond/branch_1_fun/dot_general | solution.py:8
  270.6 0.0 copy-done.1
  270.6 0.0 copy-start
  270.6 8.3 %fusion.14 = f32[1024,128]{1,0:T(8,128)S(1)} fusion(bf16[1024,8192]{1,0:T(8,128)(2,1)} %multiply_convert_fusion, bf16[8192,128]{1,0:T(8,128)(2,1)S(1)} %copy-done.1), kind=kOutput, calls=%fused_computation.22 | convolution fusion | flops 2147483648 | bytes 19398656 | tf_op jit(solution)/shard_map/cond/branch_1_fun/dot_general | solution.py:80
  278.9 8.4 %convolution_multiply_fusion = f32[8192,128]{0,1:T(8,128)S(1)} fusion(bf16[1024,8192]{1,0:T(8,128)(2,1)} %multiply_convert_fusion, bf16[1024,128]{1,0:T(8,128)(2,1)S(1)} %get-tuple-element.81), kind=kOutput, calls=%fused_computation.13 | convolution fusion | flops 2148532224 | bytes 21233664 | tf_op jit(solution)/shard_map/cond/branch_1_fun/dot_general | solution.py:14
  287.3 0.0 copy-done
  287.3 3.8 pad_maximum_fusion
  291.1 9.0 %copy.11 = f32[8192,256]{1,0:T(8,128)} copy(f32[8192,256]{0,1:T(8,128)} %get-tuple-element.102) | data formatting | bytes 16777216 | tf_op jit(solution)/shard_map/cond | solution.py:87
  300.1 0.0 reduce-scatter.2.cloned.1.call-update
  300.2 0.8 reshape.28
  301.0 143.2 %reduce-scatter.2.cloned.1.call-done = f32[128,256]{1,0:T(8,128)} async-done(((f32[8192,256]{1,0:T(8,128)}), f32[128,256]{1,0:T(8,128)}) %reduce-scatter.2.cloned.1.call-update) | async-done | bytes 131088 | tf_op jit(solution)/shard_map/reduce_scatter | solution.py:90
  444.2 0.9 convert.4
  445.1 0.6 fusion.12
  (2 shorter events, 0.1 us)
Async XLA Ops:
  7.2 85.2 %all-gather.4.cloned.1.call-start = ((), (), s32[]{:S(2)}) async-start(), calls=%async_computation.1 | async-start | bytes 2129920 | tf_op jit(solution)/shard_map/all_gather | solution.py:66
  7.9 162.2 %all-gather.6.cloned.1.call-start = ((), (), s32[]{:S(2)}) async-start(), calls=%async_computation.2 | async-start | bytes 2129920 | tf_op jit(solution)/shard_map/all_gather | solution.py:36
  8.6 435.6 %reduce-scatter.2.cloned.1.call-start = ((), (), s32[]{:S(2)}) async-start(), calls=%async_computation.3 | async-start | bytes 8519680 | tf_op jit(solution)/shard_map/reduce_scatter | solution.py:90
  170.8 47.2 %copy-start.2 = (bf16[128,1024]{1,0:T(8,128)(2,1)S(1)}, bf16[128,1024]{1,0:T(8,128)(2,1)}, u32[]{:S(2)}) copy-start(bf16[128,1024]{1,0:T(8,128)(2,1)} %param.12) | copy-start | bytes 786436
  170.8 16.0 %copy-start.3 = (bf16[8192,128]{1,0:T(8,128)(2,1)S(1)}, bf16[8192,128]{1,0:T(8,128)(2,1)}, u32[]{:S(2)}) copy-start(bf16[8192,128]{1,0:T(8,128)(2,1)} %get-tuple-element.78) | copy-start | bytes 6291460 | tf_op jit(solution)/shard_map/cond
  249.8 20.8 %copy-start.1 = (bf16[8192,128]{1,0:T(8,128)(2,1)S(1)}, bf16[8192,128]{1,0:T(8,128)(2,1)}, u32[]{:S(2)}) copy-start(bf16[8192,128]{1,0:T(8,128)(2,1)} %get-tuple-element.82) | copy-start | bytes 6291460 | tf_op jit(solution)/shard_map/cond
  270.6 16.7 %copy-start = (f32[8192,128]{0,1:T(8,128)S(1)}, f32[8192,128]{0,1:T(8,128)}, u32[]{:S(2)}) copy-start(f32[8192,128]{0,1:T(8,128)} %fusion.8) | copy-start | bytes 12582916 | tf_op jit(solution)/shard_map/cond
Sparse Core Ops, SparseCore 0:
  10.8 81.5 all-gather.3
  95.1 74.9 all-gather.5
  300.2 143.9 reduce-scatter.1
where the time goes:
time: 457 us; the launch traced here: 452 us
  waiting for transfers between devices  257 us (56%)
  matrix products  97.2 us (21%)
  blocking collectives  44.2 us (10%)
  other arithmetic  24.9 us (5%)
  between operations  15.1 us (3%)
  local copies, waits for them, and re-layouts  13.2 us (3%)
    reduce_scatter x1, waiting for transfers between devices, on_device(): lax.psum_scatter(pair_grads, ('inner', 'outer'), scatter_dimension=0, til...  143 us
    all_gather x1, waiting for transfers between devices, on_device(): lax.all_gather(value_states, ('inner', 'outer'), axis=0, tiled=True)  77.8 us
    dot_general x3, matrix products, contract_last(): lax.dot_general(left, right, (((1,), (1,)), ((), ())), preferred_element_...  51 us
    all_gather x1, blocking collectives, on_device(): lax.all_gather(positions, ('inner', 'outer'), axis=0, tiled=True)  44.2 us
    all_gather x1, waiting for transfers between devices, on_device(): lax.all_gather(key_states, ('inner', 'outer'), axis=0, tiled=True)  35.1 us
    dot_general x2, matrix products, contract_first(): lax.dot_general(left, right, (((0,), (0,)), ((), ())), preferred_element_...  24.2 us
    reduce_sum x1, other arithmetic, forward_compute_tile(): run_total = jnp.sum(weights, axis=1)  15.7 us
    dot_general x1, matrix products, forward_compute_tile(): jnp.dot(weights.astype(jnp.bfloat16), value_part, preferred_element_type=...  13.8 us
  transfers between devices with their start and end apart: 3, of which 3 were waited for; matrix products, arithmetic and copies ran while one was open for 1% of the time, Pallas kernels for 0%

commit v1 on v0

v1 whole, which is shorter than its diff:
```python
import functools

import jax
import jax.numpy as jnp
from jax import lax
from jax.experimental import pallas as pl
from jax.experimental.pallas import tpu as pltpu
from jax.sharding import PartitionSpec as P

F32 = jnp.float32
BF16 = jnp.bfloat16
AXES = ("inner", "outer")
HD = 128
HQ = 8
SPAN = 64
TOK = 128
SHARD = TOK + 16
NZ, NY, NC = 8, 4, 2
ROWS = SPAN * HQ
QB = 2 * NY
KB = 2 * NZ * NC
KEYS = KB * SPAN
CH = 256
SCALE = HD ** -0.5
SCALE2 = SCALE * 1.4426950408889634
NEG = -1e30
VMEM_LIMIT = 48 * 1024 * 1024
FROM_BELOW = (2, 0, 3, 1)
FROM_ABOVE = (1, 3, 0, 2)
FROM_FAR = (3, 2, 1, 0)


def flat(z, y, c):
    return ((z % NZ) * NY + y % NY) * NC + c


def moves(fn):
    return [
        (flat(z, y, c), flat(*fn(z, y, c)))
        for z in range(NZ)
        for y in range(NY)
        for c in range(NC)
    ]


def send(x, fn):
    return lax.ppermute(x, AXES, moves(fn))


def to_core(z, y, c):
    return z, y, 1 - c


def along_y(d):
    return lambda z, y, c: (z, y + d, c)


def along_z(d):
    return lambda z, y, c: (z + d if c == 0 else z - d, y, c)


def dot_nt(a, b):
    return lax.dot_general(a, b, (((1,), (1,)), ((), ())), preferred_element_type=F32)


def dot_nn(a, b):
    return lax.dot_general(a, b, (((1,), (0,)), ((), ())), preferred_element_type=F32)


def key_shards(own_ref, a_ref, x_ref):
    for ref, count in ((own_ref, 2), (a_ref, 7), (x_ref, 7)):
        for i in range(count):
            yield ref, i


def sort_keys(meta, refs, ks, vs):
    for s, (ref, i) in enumerate(key_shards(*refs)):
        for b in range(2):
            row = i * SHARD + b * SPAN
            dst = pl.ds(pl.multiple_of(meta[2 * s + b] * SPAN, SPAN), SPAN)
            ks[dst, :] = ref[row:row + SPAN, 0:HD]
            vs[dst, :] = ref[row:row + SPAN, HD:2 * HD]


def fill_rows(parts, out):
    for r, (ref, row) in enumerate(parts):
        for b in range(2):
            for h in range(HQ):
                at = ((r * 2 + b) * HQ + h) * SPAN
                out[at:at + SPAN, :] = ref[row + b * SPAN:row + (b + 1) * SPAN, h * HD:(h + 1) * HD]


def lead():
    u = lax.broadcasted_iota(jnp.int32, (SPAN, ROWS), 0)
    t = lax.broadcasted_iota(jnp.int32, (SPAN, ROWS), 1) % SPAN
    return u - t


def masked(meta, scores, diff, j, qid, fill):
    parts = []
    for b in range(CH // SPAN):
        gap = (qid - meta[KB + j * (CH // SPAN) + b]) * SPAN
        part = scores[b * SPAN:(b + 1) * SPAN, :]
        parts.append(jnp.where(diff <= gap, part, fill))
    return jnp.concatenate(parts, axis=0)


def bounds(meta, qb):
    full = meta[2 * KB + qb]
    every = meta[2 * KB + QB + qb]
    return full, every, meta[2 * KB + 2 * QB + qb]


def forward_kernel(meta, own, ka, kx, q0, g0, qa, qbelow, qc, gc, st, ks, vs, vt, qs, gs, sc, acc):
    sort_keys(meta, (own, ka, kx), ks, vs)
    for j in range(KEYS // HD):
        vt[0:HD, j * HD:(j + 1) * HD] = vs[j * HD:(j + 1) * HD, :].T
    vt[HD:HD + 16, :] = jnp.ones((16, KEYS), BF16)
    fill_rows(((q0, 0), (qa, 0), (qbelow, 0), (qc, 0)), qs)
    fill_rows(((g0, 0), (qa, SHARD), (qbelow, SHARD), (gc, 0)), gs)

    def block(qb, _):
        rows = pl.ds(pl.multiple_of(qb * ROWS, ROWS), ROWS)
        q = qs[rows, :]
        full, every, qid = bounds(meta, qb)
        diff = lead()

        def score(j, top, mask):
            at = pl.ds(pl.multiple_of(j * CH, CH), CH)
            s = dot_nt(ks[at, :], q) * SCALE2
            if mask:
                s = masked(meta, s, diff, j, qid, NEG)
            sc[at, :] = s
            return jnp.maximum(top, jnp.max(s.reshape(CH // 8, 8, ROWS), axis=0))

        top = jnp.full((8, ROWS), NEG, F32)
        top = lax.fori_loop(0, full, lambda j, t: score(j, t, False), top)
        top = lax.fori_loop(full, every, lambda j, t: score(j, t, True), top)
        peak = jnp.max(top, axis=0, keepdims=True)
        acc[...] = jnp.zeros_like(acc)

        def weigh(j, _):
            at = pl.ds(pl.multiple_of(j * CH, CH), CH)
            e = jnp.exp2(sc[at, :] - peak).astype(BF16)
            acc[...] += dot_nn(vt[:, at], e)
            return 0

        lax.fori_loop(0, every, weigh, 0)
        seen = peak > 0.5 * NEG
        gt = gs[rows, :].T.astype(F32)
        total = jnp.where(seen, acc[HD:HD + 1, :], 0.0)
        dots = jnp.where(seen, jnp.sum(gt * acc[0:HD, :], axis=0, keepdims=True), 0.0)
        at = pl.ds(qb, 1)
        st[0, at, :] = peak
        st[1, at, :] = total
        st[2, at, :] = dots
        return 0

    lax.fori_loop(0, QB, block, 0)


def regroup(x, order):
    return jnp.concatenate([x[2 * i:2 * i + 2, :] for i in order], axis=0)


def backward_kernel(
    meta, own, ka, kx, q0, g0, qa, qbelow, qc, gc, st0, sta, stb, stc,
    dq, dhere, daway, ks, vs, kt, qs, gs, dk, dv, qacc, lse, dlt,
):
    sort_keys(meta, (own, ka, kx), ks, vs)
    for j in range(KEYS // HD):
        kt[:, j * HD:(j + 1) * HD] = ks[j * HD:(j + 1) * HD, :].T
    fill_rows(((q0, 0), (qa, 0), (qbelow, 0), (qc, 0)), qs)
    fill_rows(((g0, 0), (qa, SHARD), (qbelow, SHARD), (gc, 0)), gs)
    same = (0, 1, 2, 3)
    sources = ((st0, same), (sta, FROM_BELOW), (stb, FROM_ABOVE), (stc, FROM_FAR))
    peaks = [regroup(s[0], o) for s, o in sources]
    top = functools.reduce(jnp.maximum, peaks)
    shares = [jnp.exp2(p - top) for p in peaks]
    total = sum(w * regroup(s[1], o) for w, (s, o) in zip(shares, sources))
    dots = sum(w * regroup(s[2], o) for w, (s, o) in zip(shares, sources))
    lse[...] = top + jnp.log2(total)
    dlt[...] = dots / total
    dk[...] = jnp.zeros_like(dk)
    dv[...] = jnp.zeros_like(dv)

    def block(qb, _):
        rows = pl.ds(pl.multiple_of(qb * ROWS, ROWS), ROWS)
        q = qs[rows, :]
        g = gs[rows, :]
        full, every, qid = bounds(meta, qb)
        diff = lead()
        row_lse = lse[pl.ds(qb, 1), :]
        row_dlt = dlt[pl.ds(qb, 1), :]
        qacc[...] = jnp.zeros_like(qacc)

        def step(j, mask):
            at = pl.ds(pl.multiple_of(j * CH, CH), CH)
            p = jnp.exp2(dot_nt(ks[at, :], q) * SCALE2 - row_lse)
            if mask:
                p = masked(meta, p, diff, j, qid, 0.0)
            ds = (p * (dot_nt(vs[at, :], g) - row_dlt)).astype(BF16)
            dv[at, :] += dot_nn(p.astype(BF16), g)
            dk[at, :] += dot_nn(ds, q)
            qacc[...] += dot_nn(kt[:, at], ds)
            return 0

        lax.fori_loop(0, full, lambda j, _: step(j, False), 0)
        lax.fori_loop(full, every, lambda j, _: step(j, True), 0)
        done = (qacc[...] * SCALE).T.astype(BF16)
        for h in range(HQ):
            dq[qb // 2, pl.ds(pl.multiple_of((qb % 2) * SPAN, SPAN), SPAN), h * HD:(h + 1) * HD] = (
                done[h * SPAN:(h + 1) * SPAN, :]
            )
        return 0

    lax.fori_loop(0, QB, block, 0)
    for s in range(2 * NZ):
        for b in range(2):
            src = pl.ds(pl.multiple_of(meta[2 * s + b] * SPAN, SPAN), SPAN)
            if s == 0:
                ref, i = dhere, 0
            elif s == 1:
                ref, i = daway, 0
            elif s < 9:
                ref, i = dhere, s - 1
            else:
                ref, i = daway, s - 8
            row = i * TOK + b * SPAN
            ref[row:row + SPAN, 0:HD] = (dk[src, :] * SCALE).astype(BF16)
            ref[row:row + SPAN, HD:2 * HD] = dv[src, :].astype(BF16)


def call(body, outs, scratch, flops):
    vmem = pl.BlockSpec(memory_space=pltpu.VMEM)
    smem = pl.BlockSpec(memory_space=pltpu.SMEM)

    def run(meta, *args):
        return pl.pallas_call(
            body,
            out_shape=outs,
            in_specs=[smem] + [vmem] * len(args),
            out_specs=jax.tree.map(lambda _: vmem, outs),
            scratch_shapes=scratch,
            compiler_params=pltpu.CompilerParams(vmem_limit_bytes=VMEM_LIMIT),
            cost_estimate=pl.CostEstimate(
                flops=flops, bytes_accessed=6 * 1024 * 1024, transcendentals=QB * ROWS * KEYS // 2
            ),
        )(meta, *args)

    return run


def shape(*dims, dtype=BF16):
    return jax.ShapeDtypeStruct(dims, dtype)


def on_device(query_states, key_states, value_states, output_grad, positions):
    own_ids = (positions[::SPAN] // SPAN).astype(BF16)
    kv = jnp.concatenate(
        [
            jnp.concatenate([key_states, value_states], axis=1),
            jnp.broadcast_to(jnp.repeat(own_ids, HD)[None, :], (16, 2 * HD)),
        ],
        axis=0,
    )
    qg = jnp.concatenate(
        [
            query_states,
            jnp.broadcast_to(jnp.repeat(own_ids, 4 * HD)[None, :], (16, HQ * HD)),
            output_grad,
        ],
        axis=0,
    )
    qa = send(qg, along_y(1))
    qb = send(qg, along_y(-1))
    qc = send(qa[:SHARD], along_y(1))
    gc = send(qb[SHARD:], along_y(-1))
    far = send(kv, along_z(4))
    pair = jnp.concatenate([kv, send(kv, to_core)], axis=0)
    near = [send(pair, along_z(d)) for d in (3, 2, 1)]
    ka = jnp.concatenate(near[::-1] + [far], axis=0)
    kx = send(ka, to_core)

    def ids_of(x):
        return x.reshape(-1, SHARD, 2 * HD)[:, TOK, ::HD].reshape(-1)

    kid = jnp.concatenate([ids_of(pair), ids_of(ka), ids_of(kx)]).astype(jnp.int32)
    qid = jnp.concatenate(
        [own_ids] + [x[TOK, :: 4 * HD] for x in (qa, qb, qc)]
    ).astype(jnp.int32)
    rank = jnp.sum((kid[None, :] < kid[:, None]).astype(jnp.int32), axis=1)
    slots = jnp.arange(KB, dtype=jnp.int32)
    in_order = jnp.sum(jnp.where(rank[None, :] == slots[:, None], kid[None, :], 0), axis=1)
    below = jnp.sum((kid[None, :] < qid[:, None]).astype(jnp.int32), axis=1)
    upto = jnp.sum((kid[None, :] <= qid[:, None]).astype(jnp.int32), axis=1)
    per = CH // SPAN
    meta = jnp.concatenate([rank, in_order, below // per, (upto + per - 1) // per, qid])

    rows = QB * ROWS
    args = (pair, ka, kx, query_states, output_grad, qa, qb, qc, gc)
    kv_scratch = [pltpu.VMEM((KEYS, HD), BF16), pltpu.VMEM((KEYS, HD), BF16)]
    q_scratch = [pltpu.VMEM((rows, HD), BF16), pltpu.VMEM((rows, HD), BF16)]
    st = call(
        forward_kernel,
        shape(3, QB, ROWS, dtype=F32),
        kv_scratch
        + [pltpu.VMEM((HD + 16, KEYS), BF16)]
        + q_scratch
        + [pltpu.VMEM((KEYS, ROWS), F32), pltpu.VMEM((HD + 16, ROWS), F32)],
        2 * rows * KEYS * HD,
    )(meta, *args)
    stats = (st, send(st, along_y(1)), send(st, along_y(-1)), send(st, along_y(2)))
    dq, here, away = call(
        backward_kernel,
        (shape(NY, TOK, HQ * HD), shape(8 * TOK, 2 * HD), shape(8 * TOK, 2 * HD)),
        kv_scratch
        + [pltpu.VMEM((HD, KEYS), BF16)]
        + q_scratch
        + [pltpu.VMEM((KEYS, HD), F32), pltpu.VMEM((KEYS, HD), F32), pltpu.VMEM((HD, ROWS), F32)]
        + [pltpu.VMEM((QB, ROWS), F32), pltpu.VMEM((QB, ROWS), F32)],
        5 * rows * KEYS * HD,
    )(meta, *args, *stats)

    terms = [dq[0], send(dq[3], along_y(2)), send(dq[1], along_y(-1)), send(dq[2], along_y(1))]
    query_grad = sum(t.astype(F32) for t in terms).astype(BF16)
    both = here.astype(F32) + send(away, to_core).astype(F32)
    out = both[TOK:].astype(BF16)
    back = [send(out[(2 * d - 2) * TOK:2 * d * TOK], along_z(-d)) for d in (3, 2, 1)]
    back_far = send(out[6 * TOK:], along_z(-4))
    found = sum(t.astype(F32) for t in back)
    cross = send(found[TOK:].astype(BF16), to_core)
    pair_grad = both[:TOK] + back_far.astype(F32) + found[:TOK] + cross.astype(F32)
    return (
        query_grad,
        pair_grad[:, :HD].astype(BF16),
        pair_grad[:, HD:].astype(BF16),
    )


def solution(mesh):
    in_specs = (
        P(("inner", "outer"), "heads"),
        P(("inner", "outer"), "heads"),
        P(("inner", "outer"), "heads"),
        P(("inner", "outer"), "heads"),
        P(("inner", "outer")),
    )
    out_specs = (
        P(("inner", "outer"), "heads"),
        P(("inner", "outer"), "heads"),
        P(("inner", "outer"), "heads"),
    )
    return jax.shard_map(
        on_device, mesh=mesh, in_specs=in_specs, out_specs=out_specs, check_vma=False
    )
```

time: 457 us -> 125 us (0.27); the launches traced: 452 us -> 127 us
  waiting for transfers between devices: 257 us -> 33.6 us
  matrix products: 97.2 us -> 0 us
  Pallas kernels: 0 us -> 48.8 us
  blocking collectives: 44.2 us -> 0 us
  starting transfers between devices: 0.11 us -> 34.6 us
  other arithmetic: 24.9 us -> 3.75 us
  between operations: 15.1 us -> 0.84 us
  local copies, waits for them, and re-layouts: 13.2 us -> 5.57 us
    reduce_scatter x1 -> x0, waiting for transfers between devices: 143 us -> none  [on_device(): lax.psum_scatter(pair_grads, ('inner', 'outer'), scatter_dimension=0, til...]
    all_gather x2 -> x0, waiting for transfers between devices: 113 us -> none  [the longest x1 77.8 us: on_device(): lax.all_gather(value_states, ('inner', 'outer'), axis=0, tiled=True)]
    dot_general x7 -> x0, matrix products: 97.2 us -> none  [the longest x3 51 us: contract_last(): lax.dot_general(left, right, (((1,), (1,)), ((), ())), preferred_element_...]
    pallas_call x0 -> x2, Pallas kernels: none -> 48.8 us  [run(): pl.pallas_call(body, out_shape=outs, in_specs=[smem] + [vmem] * len(args)...]
    all_gather x1 -> x0, blocking collectives: 44.2 us -> none  [on_device(): lax.all_gather(positions, ('inner', 'outer'), axis=0, tiled=True)]
    ppermute x0 -> x22, starting transfers between devices: none -> 34.6 us  [send(): return lax.ppermute(x, AXES, moves(fn))]
    ppermute x0 -> x22, waiting for transfers between devices: none -> 33.6 us  [send(): return lax.ppermute(x, AXES, moves(fn))]
    reduce_sum x2 -> x3, other arithmetic: 15.9 us -> 0.48 us  [the longest x1 0.18 us: on_device(): upto = jnp.sum((kid[None, :] <= qid[:, None]).astype(jnp.int32), axis=1)]
  transfers between devices with their start and end apart: 3 -> 22, of which waited for: 3 -> 9; matrix products, arithmetic and copies ran while one was open for 1% -> 5% of each run, Pallas kernels for 0% -> 0%
where the time goes in v1:
time: 125 us; the launch traced here: 127 us
  Pallas kernels  48.8 us (39%)
  starting transfers between devices  34.6 us (28%)
  waiting for transfers between devices  33.6 us (27%)
  local copies, waits for them, and re-layouts  5.57 us (4%)
  other arithmetic  3.75 us (3%)
    pallas_call x2, Pallas kernels, run(): pl.pallas_call(body, out_shape=outs, in_specs=[smem] + [vmem] * len(args)...  48.8 us
    ppermute x22, starting transfers between devices, send(): return lax.ppermute(x, AXES, moves(fn))  34.6 us
    ppermute x22, waiting for transfers between devices, send(): return lax.ppermute(x, AXES, moves(fn))  33.6 us
  transfers between devices with their start and end apart: 22, of which 9 were waited for; matrix products, arithmetic and copies ran while one was open for 5% of the time, Pallas kernels for 0%

profile of v1, /device:TPU:1, one launch (start us, length us, event | category | flops | bytes accessed | tf_op | source)
XLA Modules:
  0.0 127.1 jit_solution(8402705386109547992)
XLA Ops:
  0.6 0.7 slice.75
  1.4 0.1 broadcast_bitcast_fusion.1
  1.5 0.8 constant_dynamic-update-slice_fusion.1
  2.2 0.8 constant_dynamic-update-slice_fusion
  3.0 3.3 %collective-permute-start = (bf16[144,256]{1,0:T(8,128)(2,1)S(1)}, bf16[144,256]{1,0:T(8,128)(2,1)S(1)}, u32[]{:S(2)}, u32[]{:S(2)}) collective-permute-start(bf16[144,256]{1,0:T(8,128)(2,1)S(1)} %pad_maximum_fusion.2), channel_id=1, source_target_pairs={{0,4},{4,0},{8,12},{12,8},{16,20},{20,16},{24,28},{28,24},{32,36},... | collective-permute-start | bytes 221192 | tf_op jit(solution)/shard_map/ppermute | solution.py:47
  6.3 5.2 %collective-permute-start.4 = (bf16[144,256]{1,0:T(8,128)(2,1)S(1)}, bf16[144,256]{1,0:T(8,128)(2,1)S(1)}, u32[]{:S(2)}, u32[]{:S(2)}) collective-permute-start(bf16[144,256]{1,0:T(8,128)(2,1)S(1)} %pad_maximum_fusion.2), channel_id=1, source_target_pairs={{0,128},{4,132},{8,136},{12,140},{16,144},{20,148},{24,152},{28,15... | collective-permute-start | bytes 221192 | tf_op jit(solution)/shard_map/ppermute | solution.py:47
  11.5 0.0 collective-permute-done
  11.6 0.1 collective-permute-start.1
  11.6 0.1 broadcast_bitcast_fusion
  11.7 0.7 collective-permute-start.2
  12.5 1.9 %pad_maximum_fusion = bf16[272,1024]{1,0:T(8,128)(2,1)} fusion(bf16[128,1024]{1,0:T(8,128)(2,1)} %g0.3, bf16[16,1024]{1,0:T(8,128)(2,1)S(1)} %broadcast_in_dim.45, bf16[128,1024]{1,0:T(8,128)(2,1)} %q0.3), kind=kLoop, calls=%fused_computation.1 | loop fusion | flops 1671168 | bytes 1114112 | tf_op jit(solution)/shard_map/concatenate | solution.py:267
  14.3 2.7 %collective-permute-start.7 = (bf16[272,1024]{1,0:T(8,128)(2,1)}, bf16[272,1024]{1,0:T(8,128)(2,1)S(1)}, u32[]{:S(2)}, u32[]{:S(2)}) collective-permute-start(bf16[272,1024]{1,0:T(8,128)(2,1)} %pad_maximum_fusion), channel_id=1, source_target_pairs={{0,24},{4,28},{8,0},{12,4},{16,8},{20,12},{24,16},{28,20},{32,56},... | collective-permute-start | bytes 1671176 | tf_op jit(solution)/shard_map/ppermute | solution.py:47
  17.1 1.3 %collective-permute-done.1 = bf16[288,256]{1,0:T(8,128)(2,1)S(1)} collective-permute-done((bf16[288,256]{1,0:T(8,128)(2,1)S(1)}, bf16[288,256]{1,0:T(8,128)(2,1)S(1)}, u32[]{:S(2)}, u32[]{:S(2)}) %collective-permute-start.1) | collective-permute-done | bytes 147488 | tf_op jit(solution)/shard_map/ppermute | solution.py:47
  18.4 2.7 %collective-permute-start.3 = (bf16[288,256]{1,0:T(8,128)(2,1)S(1)}, bf16[288,256]{1,0:T(8,128)(2,1)S(1)}, u32[]{:S(2)}, u32[]{:S(2)}) collective-permute-start(bf16[288,256]{1,0:T(8,128)(2,1)S(1)} %pad_maximum_fusion.1.own), channel_id=1, source_target_pairs={{0,96},{4,164},{8,104},{12,172},{16,112},{20,180},{24,120},{28,188... | collective-permute-start | bytes 442376 | tf_op jit(solution)/shard_map/ppermute | solution.py:47
  21.1 0.0 collective-permute-done.2
  21.2 6.2 %collective-permute-done.3 = bf16[288,256]{1,0:T(8,128)(2,1)S(1)} collective-permute-done((bf16[288,256]{1,0:T(8,128)(2,1)S(1)}, bf16[288,256]{1,0:T(8,128)(2,1)S(1)}, u32[]{:S(2)}, u32[]{:S(2)}) %collective-permute-start.3) | collective-permute-done | bytes 147488 | tf_op jit(solution)/shard_map/ppermute | solution.py:47
  27.4 2.8 %collective-permute-start.5 = (bf16[1008,256]{1,0:T(8,128)(2,1)S(1)}, bf16[1008,256]{1,0:T(8,128)(2,1)S(1)}, u32[]{:S(2)}, u32[]{:S(2)}) collective-permute-start(bf16[1008,256]{1,0:T(8,128)(2,1)S(1)} %constant_dynamic-update-slice_fusion.2.ka), channel_id=1, source_target_pairs={{0,4},{4,0},{8,12},{12,8},{16,20},{20,16},{24,28},{28,24},{32,36},... | collective-permute-start | bytes 1548296 | tf_op jit(solution)/shard_map/ppermute | solution.py:47
  30.2 0.1 slice.76
  30.3 0.1 concatenate.52
  30.4 0.1 slice.77
  30.5 0.1 concatenate.54
  30.6 0.7 slice.98
  31.3 3.0 %collective-permute-start.9 = (bf16[128,1024]{1,0:T(8,128)(2,1)}, bf16[128,1024]{1,0:T(8,128)(2,1)S(1)}, u32[]{:S(2)}, u32[]{:S(2)}) collective-permute-start(bf16[128,1024]{1,0:T(8,128)(2,1)} %slice.98), channel_id=1, source_target_pairs={{0,24},{4,28},{8,0},{12,4},{16,8},{20,12},{24,16},{28,20},{32,56},... | collective-permute-start | bytes 786440 | tf_op jit(solution)/shard_map/ppermute | solution.py:47
  34.3 0.0 collective-permute-done.6.qa
  34.3 0.7 slice.97
  35.0 0.1 slice.80
  35.1 0.1 slice.79
  35.2 0.0 collective-permute-done.5.kx
  35.2 0.1 slice.78
  35.3 0.1 concatenate.55
  35.4 0.1 maximum_convert_fusion
  35.5 0.2 convert_reduce_fusion
  35.7 0.1 select_reduce_fusion
  35.8 8.9 %collective-permute-done.8.qc = bf16[144,1024]{1,0:T(8,128)(2,1)S(1)} collective-permute-done((bf16[144,1024]{1,0:T(8,128)(2,1)}, bf16[144,1024]{1,0:T(8,128)(2,1)S(1)}, u32[]{:S(2)}, u32[]{:S(2)}) %collective-permute-start.8) | collective-permute-done | bytes 294944 | tf_op jit(solution)/shard_map/ppermute | solution.py:47
  44.8 0.1 slice.82
  44.8 0.1 maximum_convert_fusion.1
  44.9 0.2 convert_reduce_fusion.1
  45.1 0.1 concatenate.62.meta
  45.2 24.3 %shard_map.76.st0 = f32[3,8,512]{2,1,0:T(8,128)S(1)} custom-call(s32[88]{0:T(128)S(1)} %concatenate.62.meta, bf16[288,256]{1,0:T(8,128)(2,1)S(1)} %pad_maximum_fusion.1.own, bf16[1008,256]{1,0:T(8,128)(2,1)S(1)} %constant_dynamic-update-slice_fusion.2.ka, bf16[1008,256]{1,0:T(8,128)(2,1)S(1)} %collective-permute-done.5.kx, bf16[128,1024]{1,0:T(8,128)(2,1)S(1)} %copy-done.1, ...), custom_call_target="tpu_custom_call" | custom-call | flops 2147483648 | bytes 6291456 | tf_op jit(solution)/shard_map/pallas_call | solution.py:239
  69.6 0.1 collective-permute-start.12
  69.7 0.1 collective-permute-start.11
  69.8 1.5 %collective-permute-start.10 = (f32[3,8,512]{2,1,0:T(8,128)S(1)}, f32[3,8,512]{2,1,0:T(8,128)S(1)}, u32[]{:S(2)}, u32[]{:S(2)}) collective-permute-start(f32[3,8,512]{2,1,0:T(8,128)S(1)} %shard_map.76.st0), channel_id=1, source_target_pairs={{0,8},{4,12},{8,16},{12,20},{16,24},{20,28},{24,0},{28,4},{32,40},... | collective-permute-start | bytes 147464 | tf_op jit(solution)/shard_map/ppermute | solution.py:47
  71.2 2.9 %collective-permute-done.12.stc = f32[3,8,512]{2,1,0:T(8,128)S(1)} collective-permute-done((f32[3,8,512]{2,1,0:T(8,128)S(1)}, f32[3,8,512]{2,1,0:T(8,128)S(1)}, u32[]{:S(2)}, u32[]{:S(2)}) %collective-permute-start.12) | collective-permute-done | bytes 49184 | tf_op jit(solution)/shard_map/ppermute | solution.py:47
  74.1 0.5 collective-permute-done.10.sta
  74.6 24.4 %shard_map.77 = (bf16[4,128,1024]{2,1,0:T(8,128)(2,1)S(1)}, bf16[1024,256]{1,0:T(8,128)(2,1)S(1)}, bf16[1024,256]{1,0:T(8,128)(2,1)S(1)}) custom-call(s32[88]{0:T(128)S(1)} %concatenate.62.meta, bf16[288,256]{1,0:T(8,128)(2,1)S(1)} %pad_maximum_fusion.1.own, bf16[1008,256]{1,0:T(8,128)(2,1)S(1)} %constant_dynamic-update-slice_fusion.2.ka, ...), custom_call_target="tpu_custom_call" | custom-call | flops 5368709120 | bytes 6291456 | tf_op jit(solution)/shard_map/pallas_call | solution.py:239
  99.1 9.1 %collective-permute-start.16 = (bf16[1024,256]{1,0:T(8,128)(2,1)S(1)}, bf16[1024,256]{1,0:T(8,128)(2,1)S(1)}, u32[]{:S(2)}, u32[]{:S(2)}) collective-permute-start(bf16[1024,256]{1,0:T(8,128)(2,1)S(1)} %get-tuple-element.8), channel_id=1, source_target_pairs={{0,4},{4,0},{8,12},{12,8},{16,20},{20,16},{24,28},{28,24},{32,36},... | collective-permute-start | bytes 1572872 | tf_op jit(solution)/shard_map/ppermute | solution.py:47
  108.1 1.5 %collective-permute-done.16 = bf16[1024,256]{1,0:T(8,128)(2,1)S(1)} collective-permute-done((bf16[1024,256]{1,0:T(8,128)(2,1)S(1)}, bf16[1024,256]{1,0:T(8,128)(2,1)S(1)}, u32[]{:S(2)}, u32[]{:S(2)}) %collective-permute-start.16) | collective-permute-done | bytes 524320 | tf_op jit(solution)/shard_map/ppermute | solution.py:47
  109.7 0.2 convert_add_fusion
  109.9 0.1 collective-permute-start.18
  110.0 0.1 collective-permute-start.20
  110.0 0.1 collective-permute-start.19
  110.1 0.1 slice_bitcast_fusion.2
  110.2 0.3 collective-permute-start.13
  110.5 0.0 collective-permute-start.15
  110.5 6.4 %collective-permute-done.18 = bf16[256,256]{1,0:T(8,128)(2,1)S(1)} collective-permute-done((bf16[256,256]{1,0:T(8,128)(2,1)S(1)}, bf16[256,256]{1,0:T(8,128)(2,1)S(1)}, u32[]{:S(2)}, u32[]{:S(2)}) %collective-permute-start.18) | collective-permute-done | bytes 131104 | tf_op jit(solution)/shard_map/ppermute | solution.py:47
  117.0 0.0 collective-permute-start.14
  117.0 1.2 collective-permute-done.20
  118.2 0.6 collective-permute-start.17
  118.8 0.0 collective-permute-done.19
  118.8 2.1 %collective-permute-start.21 = (bf16[128,256]{1,0:T(8,128)(2,1)S(1)}, bf16[128,256]{1,0:T(8,128)(2,1)S(1)}, u32[]{:S(2)}, u32[]{:S(2)}) collective-permute-start(bf16[128,256]{1,0:T(8,128)(2,1)S(1)} %slice.121), channel_id=1, source_target_pairs={{0,4},{4,0},{8,12},{12,8},{16,20},{20,16},{24,28},{28,24},{32,36},... | collective-permute-start | bytes 196616 | tf_op jit(solution)/shard_map/ppermute | solution.py:47
  121.0 4.6 %collective-permute-done.15 = bf16[128,1024]{1,0:T(8,128)(2,1)S(1)} collective-permute-done((bf16[128,1024]{1,0:T(8,128)(2,1)S(1)}, bf16[128,1024]{1,0:T(8,128)(2,1)S(1)}, u32[]{:S(2)}, u32[]{:S(2)}) %collective-permute-start.15) | collective-permute-done | bytes 262176 | tf_op jit(solution)/shard_map/ppermute | solution.py:47
  125.5 0.9 fusion.2
  126.4 0.0 collective-permute-done.17
  126.5 0.6 fusion.8
  (32 shorter events, 0.3 us)
Async XLA Ops:
  3.0 8.5 %collective-permute-start = (bf16[144,256]{1,0:T(8,128)(2,1)S(1)}, bf16[144,256]{1,0:T(8,128)(2,1)S(1)}, u32[]{:S(2)}, u32[]{:S(2)}) collective-permute-start(bf16[144,256]{1,0:T(8,128)(2,1)S(1)} %pad_maximum_fusion.2), channel_id=1, source_target_pairs={{0,4},{4,0},{8,12},{12,8},{16,20},{20,16},{24,28},{28,24},{32,36},... | collective-permute-start | bytes 221192 | tf_op jit(solution)/shard_map/ppermute | solution.py:47
  6.3 21.0 %collective-permute-start.4 = (bf16[144,256]{1,0:T(8,128)(2,1)S(1)}, bf16[144,256]{1,0:T(8,128)(2,1)S(1)}, u32[]{:S(2)}, u32[]{:S(2)}) collective-permute-start(bf16[144,256]{1,0:T(8,128)(2,1)S(1)} %pad_maximum_fusion.2), channel_id=1, source_target_pairs={{0,128},{4,132},{8,136},{12,140},{16,144},{20,148},{24,152},{28,15... | collective-permute-start | bytes 221192 | tf_op jit(solution)/shard_map/ppermute | solution.py:47
  11.6 6.8 %collective-permute-start.1 = (bf16[288,256]{1,0:T(8,128)(2,1)S(1)}, bf16[288,256]{1,0:T(8,128)(2,1)S(1)}, u32[]{:S(2)}, u32[]{:S(2)}) collective-permute-start(bf16[288,256]{1,0:T(8,128)(2,1)S(1)} %pad_maximum_fusion.1.own), channel_id=1, source_target_pairs={{0,32},{4,228},{8,40},{12,236},{16,48},{20,244},{24,56},{28,252},{... | collective-permute-start | bytes 442376 | tf_op jit(solution)/shard_map/ppermute | solution.py:47
  11.7 9.4 %collective-permute-start.2 = (bf16[288,256]{1,0:T(8,128)(2,1)S(1)}, bf16[288,256]{1,0:T(8,128)(2,1)S(1)}, u32[]{:S(2)}, u32[]{:S(2)}) collective-permute-start(bf16[288,256]{1,0:T(8,128)(2,1)S(1)} %pad_maximum_fusion.1.own), channel_id=1, source_target_pairs={{0,64},{4,196},{8,72},{12,204},{16,80},{20,212},{24,88},{28,220},{... | collective-permute-start | bytes 442376 | tf_op jit(solution)/shard_map/ppermute | solution.py:47
  14.3 30.9 %copy-start = (bf16[128,1024]{1,0:T(8,128)(2,1)S(1)}, bf16[128,1024]{1,0:T(8,128)(2,1)}, u32[]{:S(2)}) copy-start(bf16[128,1024]{1,0:T(8,128)(2,1)} %g0.3) | copy-start | bytes 786436
  14.3 30.9 %copy-start.1 = (bf16[128,1024]{1,0:T(8,128)(2,1)S(1)}, bf16[128,1024]{1,0:T(8,128)(2,1)}, u32[]{:S(2)}) copy-start(bf16[128,1024]{1,0:T(8,128)(2,1)} %q0.3) | copy-start | bytes 786436
  14.3 16.3 %collective-permute-start.7 = (bf16[272,1024]{1,0:T(8,128)(2,1)}, bf16[272,1024]{1,0:T(8,128)(2,1)S(1)}, u32[]{:S(2)}, u32[]{:S(2)}) collective-permute-start(bf16[272,1024]{1,0:T(8,128)(2,1)} %pad_maximum_fusion), channel_id=1, source_target_pairs={{0,24},{4,28},{8,0},{12,4},{16,8},{20,12},{24,16},{28,20},{32,56},... | collective-permute-start | bytes 1671176 | tf_op jit(solution)/shard_map/ppermute | solution.py:47
  17.1 17.2 %collective-permute-start.6 = (bf16[272,1024]{1,0:T(8,128)(2,1)}, bf16[272,1024]{1,0:T(8,128)(2,1)S(1)}, u32[]{:S(2)}, u32[]{:S(2)}) collective-permute-start(bf16[272,1024]{1,0:T(8,128)(2,1)} %pad_maximum_fusion), channel_id=1, source_target_pairs={{0,8},{4,12},{8,16},{12,20},{16,24},{20,28},{24,0},{28,4},{32,40},... | collective-permute-start | bytes 1671176 | tf_op jit(solution)/shard_map/ppermute | solution.py:47
  18.4 8.9 %collective-permute-start.3 = (bf16[288,256]{1,0:T(8,128)(2,1)S(1)}, bf16[288,256]{1,0:T(8,128)(2,1)S(1)}, u32[]{:S(2)}, u32[]{:S(2)}) collective-permute-start(bf16[288,256]{1,0:T(8,128)(2,1)S(1)} %pad_maximum_fusion.1.own), channel_id=1, source_target_pairs={{0,96},{4,164},{8,104},{12,172},{16,112},{20,180},{24,120},{28,188... | collective-permute-start | bytes 442376 | tf_op jit(solution)/shard_map/ppermute | solution.py:47
  27.4 7.8 %collective-permute-start.5 = (bf16[1008,256]{1,0:T(8,128)(2,1)S(1)}, bf16[1008,256]{1,0:T(8,128)(2,1)S(1)}, u32[]{:S(2)}, u32[]{:S(2)}) collective-permute-start(bf16[1008,256]{1,0:T(8,128)(2,1)S(1)} %constant_dynamic-update-slice_fusion.2.ka), channel_id=1, source_target_pairs={{0,4},{4,0},{8,12},{12,8},{16,20},{20,16},{24,28},{28,24},{32,36},... | collective-permute-start | bytes 1548296 | tf_op jit(solution)/shard_map/ppermute | solution.py:47
  31.3 13.9 %collective-permute-start.9 = (bf16[128,1024]{1,0:T(8,128)(2,1)}, bf16[128,1024]{1,0:T(8,128)(2,1)S(1)}, u32[]{:S(2)}, u32[]{:S(2)}) collective-permute-start(bf16[128,1024]{1,0:T(8,128)(2,1)} %slice.98), channel_id=1, source_target_pairs={{0,24},{4,28},{8,0},{12,4},{16,8},{20,12},{24,16},{28,20},{32,56},... | collective-permute-start | bytes 786440 | tf_op jit(solution)/shard_map/ppermute | solution.py:47
  35.0 9.7 %collective-permute-start.8 = (bf16[144,1024]{1,0:T(8,128)(2,1)}, bf16[144,1024]{1,0:T(8,128)(2,1)S(1)}, u32[]{:S(2)}, u32[]{:S(2)}) collective-permute-start(bf16[144,1024]{1,0:T(8,128)(2,1)} %slice.97), channel_id=1, source_target_pairs={{0,8},{4,12},{8,16},{12,20},{16,24},{20,28},{24,0},{28,4},{32,40},... | collective-permute-start | bytes 884744 | tf_op jit(solution)/shard_map/ppermute | solution.py:47
  69.6 4.6 %collective-permute-start.12 = (f32[3,8,512]{2,1,0:T(8,128)S(1)}, f32[3,8,512]{2,1,0:T(8,128)S(1)}, u32[]{:S(2)}, u32[]{:S(2)}) collective-permute-start(f32[3,8,512]{2,1,0:T(8,128)S(1)} %shard_map.76.st0), channel_id=1, source_target_pairs={{0,16},{4,20},{8,24},{12,28},{16,0},{20,4},{24,8},{28,12},{32,48},... | collective-permute-start | bytes 147464 | tf_op jit(solution)/shard_map/ppermute | solution.py:47
  69.7 4.5 %collective-permute-start.11 = (f32[3,8,512]{2,1,0:T(8,128)S(1)}, f32[3,8,512]{2,1,0:T(8,128)S(1)}, u32[]{:S(2)}, u32[]{:S(2)}) collective-permute-start(f32[3,8,512]{2,1,0:T(8,128)S(1)} %shard_map.76.st0), channel_id=1, source_target_pairs={{0,24},{4,28},{8,0},{12,4},{16,8},{20,12},{24,16},{28,20},{32,56},... | collective-permute-start | bytes 147464 | tf_op jit(solution)/shard_map/ppermute | solution.py:47
  69.8 4.9 %collective-permute-start.10 = (f32[3,8,512]{2,1,0:T(8,128)S(1)}, f32[3,8,512]{2,1,0:T(8,128)S(1)}, u32[]{:S(2)}, u32[]{:S(2)}) collective-permute-start(f32[3,8,512]{2,1,0:T(8,128)S(1)} %shard_map.76.st0), channel_id=1, source_target_pairs={{0,8},{4,12},{8,16},{12,20},{16,24},{20,28},{24,0},{28,4},{32,40},... | collective-permute-start | bytes 147464 | tf_op jit(solution)/shard_map/ppermute | solution.py:47
  99.1 10.6 %collective-permute-start.16 = (bf16[1024,256]{1,0:T(8,128)(2,1)S(1)}, bf16[1024,256]{1,0:T(8,128)(2,1)S(1)}, u32[]{:S(2)}, u32[]{:S(2)}) collective-permute-start(bf16[1024,256]{1,0:T(8,128)(2,1)S(1)} %get-tuple-element.8), channel_id=1, source_target_pairs={{0,4},{4,0},{8,12},{12,8},{16,20},{20,16},{24,28},{28,24},{32,36},... | collective-permute-start | bytes 1572872 | tf_op jit(solution)/shard_map/ppermute | solution.py:47
  109.9 7.1 %collective-permute-start.18 = (bf16[256,256]{1,0:T(8,128)(2,1)S(1)}, bf16[256,256]{1,0:T(8,128)(2,1)S(1)}, u32[]{:S(2)}, u32[]{:S(2)}) collective-permute-start(bf16[256,256]{1,0:T(8,128)(2,1)S(1)} %get-tuple-element.16), channel_id=1, source_target_pairs={{0,160},{4,100},{8,168},{12,108},{16,176},{20,116},{24,184},{28,12... | collective-permute-start | bytes 393224 | tf_op jit(solution)/shard_map/ppermute | solution.py:47
  110.0 8.2 %collective-permute-start.20 = (bf16[256,256]{1,0:T(8,128)(2,1)S(1)}, bf16[256,256]{1,0:T(8,128)(2,1)S(1)}, u32[]{:S(2)}, u32[]{:S(2)}) collective-permute-start(bf16[256,256]{1,0:T(8,128)(2,1)S(1)} %get-tuple-element.17), channel_id=1, source_target_pairs={{0,224},{4,36},{8,232},{12,44},{16,240},{20,52},{24,248},{28,60},{... | collective-permute-start | bytes 393224 | tf_op jit(solution)/shard_map/ppermute | solution.py:47
  110.0 8.7 %collective-permute-start.19 = (bf16[256,256]{1,0:T(8,128)(2,1)S(1)}, bf16[256,256]{1,0:T(8,128)(2,1)S(1)}, u32[]{:S(2)}, u32[]{:S(2)}) collective-permute-start(bf16[256,256]{1,0:T(8,128)(2,1)S(1)} %get-tuple-element.18), channel_id=1, source_target_pairs={{0,192},{4,68},{8,200},{12,76},{16,208},{20,84},{24,216},{28,92},{... | collective-permute-start | bytes 393224 | tf_op jit(solution)/shard_map/ppermute | solution.py:47
  110.2 10.8 %collective-permute-start.13 = (bf16[128,1024]{1,0:T(8,128)(2,1)S(1)}, bf16[128,1024]{1,0:T(8,128)(2,1)S(1)}, u32[]{:S(2)}, u32[]{:S(2)}) collective-permute-start(bf16[128,1024]{1,0:T(8,128)(2,1)S(1)} %get-tuple-element.13), channel_id=1, source_target_pairs={{0,16},{4,20},{8,24},{12,28},{16,0},{20,4},{24,8},{28,12},{32,48},... | collective-permute-start | bytes 786440 | tf_op jit(solution)/shard_map/ppermute | solution.py:47
  110.5 15.0 %collective-permute-start.15 = (bf16[128,1024]{1,0:T(8,128)(2,1)S(1)}, bf16[128,1024]{1,0:T(8,128)(2,1)S(1)}, u32[]{:S(2)}, u32[]{:S(2)}) collective-permute-start(bf16[128,1024]{1,0:T(8,128)(2,1)S(1)} %get-tuple-element.14), channel_id=1, source_target_pairs={{0,8},{4,12},{8,16},{12,20},{16,24},{20,28},{24,0},{28,4},{32,40},... | collective-permute-start | bytes 786440 | tf_op jit(solution)/shard_map/ppermute | solution.py:47
  117.0 8.6 %collective-permute-start.14 = (bf16[128,1024]{1,0:T(8,128)(2,1)S(1)}, bf16[128,1024]{1,0:T(8,128)(2,1)S(1)}, u32[]{:S(2)}, u32[]{:S(2)}) collective-permute-start(bf16[128,1024]{1,0:T(8,128)(2,1)S(1)} %get-tuple-element.15), channel_id=1, source_target_pairs={{0,24},{4,28},{8,0},{12,4},{16,8},{20,12},{24,16},{28,20},{32,56},... | collective-permute-start | bytes 786440 | tf_op jit(solution)/shard_map/ppermute | solution.py:47
  118.2 8.3 %collective-permute-start.17 = (bf16[128,256]{1,0:T(8,128)(2,1)S(1)}, bf16[128,256]{1,0:T(8,128)(2,1)S(1)}, u32[]{:S(2)}, u32[]{:S(2)}) collective-permute-start(bf16[128,256]{1,0:T(8,128)(2,1)S(1)} %slice.100), channel_id=1, source_target_pairs={{0,128},{4,132},{8,136},{12,140},{16,144},{20,148},{24,152},{28,15... | collective-permute-start | bytes 196616 | tf_op jit(solution)/shard_map/ppermute | solution.py:47
  118.8 7.6 %collective-permute-start.21 = (bf16[128,256]{1,0:T(8,128)(2,1)S(1)}, bf16[128,256]{1,0:T(8,128)(2,1)S(1)}, u32[]{:S(2)}, u32[]{:S(2)}) collective-permute-start(bf16[128,256]{1,0:T(8,128)(2,1)S(1)} %slice.121), channel_id=1, source_target_pairs={{0,4},{4,0},{8,12},{12,8},{16,20},{20,16},{24,28},{28,24},{32,36},... | collective-permute-start | bytes 196616 | tf_op jit(solution)/shard_map/ppermute | solution.py:47
